TPU v7x, 32 devices: a whole 2x2x4 slice. The times are simulated.
32 devices in a mesh: grp: 2 (over x), row: 16 (over z, y, core).
Axes of the slice: x: 2, y: 2, z: 4, core: 2. Of those that a mesh axis runs over, the one named last changes fastest.
Arguments:
- matrix: bfloat16 [32, 2048, 16384], P(('grp', 'row')), parts along dimension 0, may hold values from -1 to 1
- probes: bfloat16 [16384, 128], P(('grp', 'row')), parts along dimension 0, may hold values from -6 to 6
Outputs:
- basis_out: bfloat16 [16384, 128], P(('grp', 'row')), parts along dimension 0
- sketch_out: bfloat16 [32, 4096, 128], P(('grp', 'row')), parts along dimension 0
There are 2 independent parts, one for each index of `grp`. A program takes and returns all parts, laid end to end along the dimension named above; each array names one. Nothing has to cross between parts.
All inputs are finite; a program needn't handle non-finite values.
Results may differ from a plain program's by a relative error of at most 0.012.
Values may be sent and summed in bfloat16 or wider, within the bound.
A program may use at most 192 MiB of HBM per device.

v0:
```python
import math
import jax
import jax.numpy as jnp
from jax import lax
from jax.sharding import PartitionSpec as P

GRID_ROWS = 4
ITERS = 2


def from_partner(shard, axis, bit):
    return lax.ppermute(shard, axis, [(i, i ^ 1 << bit) for i in range(lax.axis_size(axis))])


def orthonormal(product, gram_matrix, rescale):
    factor = jnp.linalg.cholesky(gram_matrix)
    solved = lax.linalg.triangular_solve(
        factor, product, left_side=False, lower=True, transpose_a=True
    )
    return (solved * rescale).astype(jnp.bfloat16)


def digit_set(device, level):
    return device // 2**level % 2 == 1


def per_device(matrix, probes):
    tile_block = matrix[0]
    tile_rows = tile_block.shape[0]
    grid_cols = lax.axis_size("row") // GRID_ROWS
    col_levels = grid_cols.bit_length() - 1
    row_levels = GRID_ROWS.bit_length() - 1
    device = lax.axis_index("row")
    rescale = math.sqrt(GRID_ROWS * tile_rows)
    current = probes
    sketch_block = None
    for iteration in range(ITERS):
        panel = current
        for level in range(col_levels):
            other = from_partner(panel, "row", level)
            panel = jnp.where(
                digit_set(device, level),
                jnp.concatenate([other, panel], 0),
                jnp.concatenate([panel, other], 0),
            )
        partial_value = lax.dot_general(
            tile_block, panel, (((0,), (0,)), ((), ())), preferred_element_type=jnp.float32
        )
        for level in range(row_levels):
            partial_value = partial_value + from_partner(
                partial_value.astype(jnp.bfloat16), "row", col_levels + level
            ).astype(partial_value.dtype)
        sketch = partial_value.astype(jnp.bfloat16)
        share_rows = sketch.shape[0] // GRID_ROWS
        grid_row = device // grid_cols
        sketch_block = lax.dynamic_slice_in_dim(sketch, grid_row * share_rows, share_rows, 0)
        image = jnp.dot(tile_block, sketch, preferred_element_type=jnp.float32)
        for level in reversed(range(col_levels)):
            half_rows = image.shape[0] // 2
            lower_part = image[:half_rows]
            upper_part = image[half_rows:]
            upward = digit_set(device, level)
            sent = jnp.where(upward, lower_part, upper_part)
            kept = jnp.where(upward, upper_part, lower_part)
            image = kept + from_partner(sent.astype(jnp.bfloat16), "row", level).astype(sent.dtype)
        local_gram = jnp.dot(
            image.T, image, precision=lax.Precision.HIGHEST, preferred_element_type=jnp.float32
        )
        gram_matrix = lax.psum(local_gram, "row")
        current = orthonormal(image, gram_matrix, rescale)
    return (current, sketch_block[None])


def solution(mesh):
    placed = (P(("grp", "row"), None, None), P(("grp", "row"), None))
    return jax.shard_map(
        per_device,
        mesh=mesh,
        in_specs=placed,
        out_specs=(P(("grp", "row"), None), P(("grp", "row"), None, None)),
        check_vma=False,
    )
```

profile of v0, /device:TPU:8, one launch (start us, length us, event | category | flops | bytes accessed | tf_op | source)
XLA Modules:
  0.0 968.9 jit_solution(17788045940890955766)
XLA Ops:
  9.7 1.6 collective-permute-start.1
  11.3 6.8 collective-permute-done.1
  18.2 28.6 %fusion.50 = (bf16[16384,128]{0,1:T(8,128)(2,1)}, f32[16384,128]{0,1:T(8,128)}) fusion(bf16[1,2048,16384]{2,1,0:T(8,128)(2,1)} %param.5, bf16[1024,128]{0,1:T(8,128)(2,1)S(1)} %maximum_select_fusion.4, bf16[1024,128]{0,1:T(8,128)(2,1)S(1)} %collective-permute-done.1, pred[]{:T(512)S(6)} %eq.22), kind=kOutput, calls=%fused_computation.70 | convolution fusion | flops 8594391040 | bytes 80216064 | tf_op jit(solution)/shard_map/dot_general | solution.py:46
  47.0 91.8 %collective-permute-done.2 = bf16[16384,128]{0,1:T(8,128)(2,1)S(1)} collective-permute-done((bf16[16384,128]{0,1:T(8,128)(2,1)}, bf16[16384,128]{0,1:T(8,128)(2,1)S(1)}, u32[]{:S(2)}, u32[]{:S(2)}) %collective-permute-start.2) | collective-permute-done | bytes 4194336 | tf_op jit(solution)/shard_map/ppermute | solution.py:12
  138.8 5.7 fusion.14
  144.5 2.7 collective-permute-start.3
  147.1 178.2 %collective-permute-done.3 = bf16[16384,128]{0,1:T(8,128)(2,1)} collective-permute-done((bf16[16384,128]{0,1:T(8,128)(2,1)S(1)}, bf16[16384,128]{0,1:T(8,128)(2,1)}, u32[]{:S(2)}, u32[]{:S(2)}) %collective-permute-start.3) | collective-permute-done | bytes 4194336 | tf_op jit(solution)/shard_map/ppermute | solution.py:12
  325.3 33.8 %fusion.16 = f32[2048,128]{0,1:T(8,128)S(1)} fusion(bf16[1,2048,16384]{2,1,0:T(8,128)(2,1)} %param.5, bf16[16384,128]{0,1:T(8,128)(2,1)} %collective-permute-done.3, f32[16384,128]{0,1:T(8,128)} %get-tuple-element.9, bf16[16384,128]{0,1:T(8,128)(2,1)} %copy-done), kind=kOutput, calls=%fused_computation.16 | convolution fusion | flops 8600420352 | bytes 84934656 | tf_op jit(solution)/shard_map/dot_general | solution.py:57
  359.2 1.6 collective-permute-start.4
  360.8 6.7 collective-permute-done.4
  370.3 89.0 %all-reduce.3.cloned.1.call-done = f32[128,128]{0,1:T(8,128)} async-done(((f32[128,128]{0,1:T(8,128)}), f32[128,128]{0,1:T(8,128)}) %all-reduce.3.cloned.1.call-update) | async-done | bytes 65552 | tf_op jit(solution)/shard_map/psum | solution.py:69
  461.1 11.7 %cholesky.44 = f32[128,128]{1,0:T(8,128)S(1)} custom-call(f32[128,128]{1,0:T(8,128)S(1)} %fusion.43), custom_call_target="Cholesky" | custom-call | tf_op jit(solution)/shard_map/jit(cholesky)/cholesky | solution.py:16
  474.2 9.8 %custom-call.6 = f32[1,128,128]{1,2,0:T(8,128)S(1)} custom-call(f32[1,128,128]{2,1,0:T(8,128)S(1)} %fusion.38), custom_call_target="InvertDiagBlocksLowerTriangular" | custom-call | tf_op jit(solution)/shard_map/triangular_solve/custom-call.0 | solution.py:17
  486.6 7.8 collective-permute-done.7
  494.4 28.6 %fusion.51 = (bf16[16384,128]{0,1:T(8,128)(2,1)}, f32[16384,128]{0,1:T(8,128)}) fusion(bf16[1,2048,16384]{2,1,0:T(8,128)(2,1)} %param.5, bf16[1024,128]{0,1:T(8,128)(2,1)S(1)} %maximum_select_fusion.5, bf16[1024,128]{0,1:T(8,128)(2,1)S(1)} %collective-permute-done.7, pred[]{:T(512)S(6)} %eq.22), kind=kOutput, calls=%fused_computation.71 | convolution fusion | flops 8594391040 | bytes 80216064 | tf_op jit(solution)/shard_map/dot_general | solution.py:46
  523.0 92.0 %collective-permute-done.8 = bf16[16384,128]{0,1:T(8,128)(2,1)S(1)} collective-permute-done((bf16[16384,128]{0,1:T(8,128)(2,1)}, bf16[16384,128]{0,1:T(8,128)(2,1)S(1)}, u32[]{:S(2)}, u32[]{:S(2)}) %collective-permute-start.8) | collective-permute-done | bytes 4194336 | tf_op jit(solution)/shard_map/ppermute | solution.py:12
  615.0 4.4 fusion.15
  620.9 178.3 %collective-permute-done.9 = bf16[16384,128]{0,1:T(8,128)(2,1)} collective-permute-done((bf16[16384,128]{0,1:T(8,128)(2,1)S(1)}, bf16[16384,128]{0,1:T(8,128)(2,1)}, u32[]{:S(2)}, u32[]{:S(2)}) %collective-permute-start.9) | collective-permute-done | bytes 4194336 | tf_op jit(solution)/shard_map/ppermute | solution.py:12
  799.2 8.2 add_convert_fusion
  807.4 29.7 %fusion.19 = f32[2048,128]{0,1:T(8,128)S(1)} fusion(bf16[16384,128]{0,1:T(8,128)(2,1)} %add_convert_fusion, bf16[1,2048,16384]{2,1,0:T(8,128)(2,1)} %param.5), kind=kOutput, calls=%fused_computation.17 | convolution fusion | flops 8589934592 | bytes 72351744 | tf_op jit(solution)/shard_map/dot_general | solution.py:57
  837.6 7.8 collective-permute-done.10
  850.6 85.7 %all-reduce.5.cloned.1.call-done = f32[128,128]{0,1:T(8,128)} async-done(((f32[128,128]{0,1:T(8,128)}), f32[128,128]{0,1:T(8,128)}) %all-reduce.5.cloned.1.call-update) | async-done | bytes 65552 | tf_op jit(solution)/shard_map/psum | solution.py:69
  938.0 11.7 %cholesky.55 = f32[128,128]{1,0:T(8,128)S(1)} custom-call(f32[128,128]{1,0:T(8,128)S(1)} %fusion.41), custom_call_target="Cholesky" | custom-call | tf_op jit(solution)/shard_map/jit(cholesky)/cholesky | solution.py:16
  951.1 9.8 %custom-call.7 = f32[1,128,128]{1,2,0:T(8,128)S(1)} custom-call(f32[1,128,128]{2,1,0:T(8,128)S(1)} %fusion.39), custom_call_target="InvertDiagBlocksLowerTriangular" | custom-call | tf_op jit(solution)/shard_map/triangular_solve/custom-call.0 | solution.py:17
  (45 shorter events, 22.7 us)
Async XLA Ops:
  7.2 452.2 %all-reduce.3.cloned.1.call-start = ((), (), s32[]{:S(2)}) async-start(), calls=%async_computation | async-start | bytes 131072 | tf_op jit(solution)/shard_map/psum | solution.py:69
  8.2 1.4 collective-permute-start
  9.7 8.4 collective-permute-start.1
  46.7 92.0 %collective-permute-start.2 = (bf16[16384,128]{0,1:T(8,128)(2,1)}, bf16[16384,128]{0,1:T(8,128)(2,1)S(1)}, u32[]{:S(2)}, u32[]{:S(2)}) collective-permute-start(bf16[16384,128]{0,1:T(8,128)(2,1)} %get-tuple-element.8), channel_id=1, source_target_pairs={{0,4},{1,5},{2,6},{3,7},{4,0},{5,1},{6,2},{7,3},{8,12},{9,13},{10,... | collective-permute-start | bytes 12582920 | tf_op jit(solution)/shard_map/ppermute | solution.py:12
  138.8 5.7 copy-start
  144.5 180.8 %collective-permute-start.3 = (bf16[16384,128]{0,1:T(8,128)(2,1)S(1)}, bf16[16384,128]{0,1:T(8,128)(2,1)}, u32[]{:S(2)}, u32[]{:S(2)}) collective-permute-start(bf16[16384,128]{0,1:T(8,128)(2,1)S(1)} %fusion.14), channel_id=1, source_target_pairs={{0,8},{1,9},{2,10},{3,11},{4,12},{5,13},{6,14},{7,15},{8,0},{9,1},... | collective-permute-start | bytes 12582920 | tf_op jit(solution)/shard_map/ppermute | solution.py:12
  359.2 8.3 collective-permute-start.4
  367.6 1.4 collective-permute-start.5
  370.1 566.2 %all-reduce.5.cloned.1.call-start = ((), (), s32[]{:S(2)}) async-start(), calls=%async_computation.1 | async-start | bytes 131072 | tf_op jit(solution)/shard_map/psum | solution.py:69
  484.4 1.4 collective-permute-start.6
  485.9 8.4 collective-permute-start.7
  523.0 92.0 %collective-permute-start.8 = (bf16[16384,128]{0,1:T(8,128)(2,1)}, bf16[16384,128]{0,1:T(8,128)(2,1)S(1)}, u32[]{:S(2)}, u32[]{:S(2)}) collective-permute-start(bf16[16384,128]{0,1:T(8,128)(2,1)} %get-tuple-element.10), channel_id=1, source_target_pairs={{0,4},{1,5},{2,6},{3,7},{4,0},{5,1},{6,2},{7,3},{8,12},{9,13},{10,... | collective-permute-start | bytes 12582920 | tf_op jit(solution)/shard_map/ppermute | solution.py:12
  619.4 179.8 %collective-permute-start.9 = (bf16[16384,128]{0,1:T(8,128)(2,1)S(1)}, bf16[16384,128]{0,1:T(8,128)(2,1)}, u32[]{:S(2)}, u32[]{:S(2)}) collective-permute-start(bf16[16384,128]{0,1:T(8,128)(2,1)S(1)} %fusion.15), channel_id=1, source_target_pairs={{0,8},{1,9},{2,10},{3,11},{4,12},{5,13},{6,14},{7,15},{8,0},{9,1},... | collective-permute-start | bytes 12582920 | tf_op jit(solution)/shard_map/ppermute | solution.py:12
  837.1 8.3 collective-permute-start.10
  845.5 1.4 collective-permute-start.11
Sparse Core Ops, SparseCore 0:
  370.2 89.0 all-reduce.2
  848.1 88.1 all-reduce.4
where the time goes:
time: 970 us; the launch traced here: 969 us
  waiting for transfers between devices  749 us (77%)
  matrix products  124 us (13%)
  other arithmetic  66.2 us (7%)
  between operations  14.3 us (1%)
    ppermute x12, waiting for transfers between devices, from_partner(): lax.ppermute(shard, axis, [(i, i ^ 1 << bit) for i in range(lax.axis_size...  575 us
    psum x2, waiting for transfers between devices, per_device(): gram_matrix = lax.psum(local_gram, 'row')  175 us
    dot_general x2, matrix products, per_device(): image = jnp.dot(tile_block, sketch, preferred_element_type=jnp.float32)  63.5 us
    dot_general x2, matrix products, per_device(): lax.dot_general(tile_block, panel, (((0,), (0,)), ((), ())), preferred_el...  57.2 us
    another operation x6, other arithmetic, orthonormal(): factor = jnp.linalg.cholesky(gram_matrix)  24.8 us
    another operation x4, other arithmetic, orthonormal(): lax.linalg.triangular_solve(factor, product, left_side=False, lower=True,...  20.9 us
  transfers between devices with their start and end apart: 14, of which 14 were waited for; matrix products, arithmetic and copies ran while one was open for 0% of the time, Pallas kernels for 0%

commit v1 on v0

--- a/solution.py
+++ b/solution.py
@@ -66,7 +66,10 @@
         local_gram = jnp.dot(
             image.T, image, precision=lax.Precision.HIGHEST, preferred_element_type=jnp.float32
         )
-        gram_matrix = lax.psum(local_gram, "row")
+        size, gram_matrix = (lax.axis_size("row"), local_gram)
+        for far in [1 << k for k in range(size.bit_length() - 1)]:
+            pairs = [(i_2, i_2 ^ far) for i_2 in range(size)]
+            gram_matrix = gram_matrix + lax.ppermute(gram_matrix, "row", pairs)
         current = orthonormal(image, gram_matrix, rescale)
     return (current, sketch_block[None])
 

time: 970 us -> 809 us (0.83)
  waiting for transfers between devices: 749 us -> 589 us
  starting transfers between devices: 9.21 us -> 25.9 us
  between operations: 14.3 us -> 0.93 us
    psum x2 -> x0, waiting for transfers between devices: 175 us -> none  [per_device(): gram_matrix = lax.psum(local_gram, 'row')]
    ppermute x0 -> x8, waiting for transfers between devices: none -> 16.7 us  [per_device(): gram_matrix = gram_matrix + lax.ppermute(gram_matrix, 'row', pairs)]
    ppermute x0 -> x8, starting transfers between devices: none -> 12.6 us  [per_device(): gram_matrix = gram_matrix + lax.ppermute(gram_matrix, 'row', pairs)]
  transfers between devices with their start and end apart: 14 -> 20, of which waited for: 14 -> 19; matrix products, arithmetic and copies ran while one was open for 0% -> 0% of each run, Pallas kernels for 0% -> 0%
where the time goes in v1:
time: 809 us; the launch traced here: 807 us
  waiting for transfers between devices  589 us (73%)
  matrix products  122 us (15%)
  other arithmetic  64.6 us (8%)
  starting transfers between devices  25.9 us (3%)
    ppermute x12, waiting for transfers between devices, from_partner(): lax.ppermute(shard, axis, [(i, i ^ 1 << bit) for i in range(lax.axis_size...  572 us
    dot_general x2, matrix products, per_device(): image = jnp.dot(tile_block, sketch, preferred_element_type=jnp.float32)  63.7 us
    dot_general x2, matrix products, per_device(): lax.dot_general(tile_block, panel, (((0,), (0,)), ((), ())), preferred_el...  57.1 us
    another operation x6, other arithmetic, orthonormal(): factor = jnp.linalg.cholesky(gram_matrix)  24.8 us
    another operation x4, other arithmetic, orthonormal(): lax.linalg.triangular_solve(factor, product, left_side=False, lower=True,...  20.9 us
    ppermute x8, waiting for transfers between devices, per_device(): gram_matrix = gram_matrix + lax.ppermute(gram_matrix, 'row', pairs)  16.7 us
  transfers between devices with their start and end apart: 20, of which 19 were waited for; matrix products, arithmetic and copies ran while one was open for 0% of the time, Pallas kernels for 0%

profile of v1, /device:TPU:8, one launch (start us, length us, event | category | flops | bytes accessed | tf_op | source)
XLA Modules:
  0.0 807.0 jit_solution(16915393175166134201)
XLA Ops:
  4.7 6.8 collective-permute-done.1
  11.6 28.5 %fusion.50 = (bf16[16384,128]{0,1:T(8,128)(2,1)}, f32[16384,128]{0,1:T(8,128)}) fusion(bf16[1,2048,16384]{2,1,0:T(8,128)(2,1)} %param.5, bf16[1024,128]{0,1:T(8,128)(2,1)S(1)} %maximum_select_fusion.4, bf16[1024,128]{0,1:T(8,128)(2,1)S(1)} %collective-permute-done.1, pred[]{:T(512)S(6)} %eq.22), kind=kOutput, calls=%fused_computation.70 | convolution fusion | flops 8594391040 | bytes 80216064 | tf_op jit(solution)/shard_map/dot_general | solution.py:46
  40.3 91.8 %collective-permute-done.2 = bf16[16384,128]{0,1:T(8,128)(2,1)S(1)} collective-permute-done((bf16[16384,128]{0,1:T(8,128)(2,1)}, bf16[16384,128]{0,1:T(8,128)(2,1)S(1)}, u32[]{:S(2)}, u32[]{:S(2)}) %collective-permute-start.2) | collective-permute-done | bytes 4194336 | tf_op jit(solution)/shard_map/ppermute | solution.py:12
  132.1 5.7 fusion.14
  140.5 178.2 %collective-permute-done.3 = bf16[16384,128]{0,1:T(8,128)(2,1)} collective-permute-done((bf16[16384,128]{0,1:T(8,128)(2,1)S(1)}, bf16[16384,128]{0,1:T(8,128)(2,1)}, u32[]{:S(2)}, u32[]{:S(2)}) %collective-permute-start.3) | collective-permute-done | bytes 4194336 | tf_op jit(solution)/shard_map/ppermute | solution.py:12
  318.7 34.0 %fusion.16 = f32[2048,128]{0,1:T(8,128)S(1)} fusion(bf16[1,2048,16384]{2,1,0:T(8,128)(2,1)} %param.5, bf16[16384,128]{0,1:T(8,128)(2,1)} %collective-permute-done.3, f32[16384,128]{0,1:T(8,128)} %get-tuple-element.9, bf16[16384,128]{0,1:T(8,128)(2,1)} %copy-done), kind=kOutput, calls=%fused_computation.16 | convolution fusion | flops 8600420352 | bytes 84934656 | tf_op jit(solution)/shard_map/dot_general | solution.py:57
  354.3 6.7 collective-permute-done.4
  370.0 3.0 collective-permute-done.8
  373.0 3.5 collective-permute-start.9
  378.9 11.7 %cholesky.44 = f32[128,128]{1,0:T(8,128)S(1)} custom-call(f32[128,128]{1,0:T(8,128)S(1)} %fusion.43), custom_call_target="Cholesky" | custom-call | tf_op jit(solution)/shard_map/jit(cholesky)/cholesky | solution.py:16
  392.0 9.8 %custom-call.6 = f32[1,128,128]{1,2,0:T(8,128)S(1)} custom-call(f32[1,128,128]{2,1,0:T(8,128)S(1)} %fusion.38), custom_call_target="InvertDiagBlocksLowerTriangular" | custom-call | tf_op jit(solution)/shard_map/triangular_solve/custom-call.0 | solution.py:17
  405.3 6.8 collective-permute-done.11
  412.2 28.5 %fusion.51 = (bf16[16384,128]{0,1:T(8,128)(2,1)}, f32[16384,128]{0,1:T(8,128)}) fusion(bf16[1,2048,16384]{2,1,0:T(8,128)(2,1)} %param.5, bf16[1024,128]{0,1:T(8,128)(2,1)S(1)} %maximum_select_fusion.5, bf16[1024,128]{0,1:T(8,128)(2,1)S(1)} %collective-permute-done.11, pred[]{:T(512)S(6)} %eq.22), kind=kOutput, calls=%fused_computation.71 | convolution fusion | flops 8594391040 | bytes 80216064 | tf_op jit(solution)/shard_map/dot_general | solution.py:46
  441.4 91.3 %collective-permute-done.12 = bf16[16384,128]{0,1:T(8,128)(2,1)S(1)} collective-permute-done((bf16[16384,128]{0,1:T(8,128)(2,1)}, bf16[16384,128]{0,1:T(8,128)(2,1)S(1)}, u32[]{:S(2)}, u32[]{:S(2)}) %collective-permute-start.12) | collective-permute-done | bytes 4194336 | tf_op jit(solution)/shard_map/ppermute | solution.py:12
  532.7 4.4 fusion.15
  537.1 3.1 collective-permute-start.13
  540.3 178.3 %collective-permute-done.13 = bf16[16384,128]{0,1:T(8,128)(2,1)} collective-permute-done((bf16[16384,128]{0,1:T(8,128)(2,1)S(1)}, bf16[16384,128]{0,1:T(8,128)(2,1)}, u32[]{:S(2)}, u32[]{:S(2)}) %collective-permute-start.13) | collective-permute-done | bytes 4194336 | tf_op jit(solution)/shard_map/ppermute | solution.py:12
  718.5 8.2 %add_convert_fusion = bf16[16384,128]{0,1:T(8,128)(2,1)} fusion(bf16[16384,128]{0,1:T(8,128)(2,1)} %collective-permute-done.13, f32[16384,128]{0,1:T(8,128)} %get-tuple-element.11, bf16[16384,128]{0,1:T(8,128)(2,1)S(1)} %collective-permute-done.12), kind=kLoop, calls=%fused_computation.10 | loop fusion | flops 10485760 | bytes 20971520 | tf_op jit(solution)/shard_map/convert_element_type | solution.py:53
  726.7 29.7 %fusion.19 = f32[2048,128]{0,1:T(8,128)S(1)} fusion(bf16[16384,128]{0,1:T(8,128)(2,1)} %add_convert_fusion, bf16[1,2048,16384]{2,1,0:T(8,128)(2,1)} %param.5), kind=kOutput, calls=%fused_computation.17 | convolution fusion | flops 8589934592 | bytes 72351744 | tf_op jit(solution)/shard_map/dot_general | solution.py:57
  758.0 6.7 collective-permute-done.14
  772.9 3.8 collective-permute-done.18
  776.7 3.6 collective-permute-start.19
  783.0 11.7 %cholesky.55 = f32[128,128]{1,0:T(8,128)S(1)} custom-call(f32[128,128]{1,0:T(8,128)S(1)} %fusion.41), custom_call_target="Cholesky" | custom-call | tf_op jit(solution)/shard_map/jit(cholesky)/cholesky | solution.py:16
  796.0 9.8 %custom-call.7 = f32[1,128,128]{1,2,0:T(8,128)S(1)} custom-call(f32[1,128,128]{2,1,0:T(8,128)S(1)} %fusion.39), custom_call_target="InvertDiagBlocksLowerTriangular" | custom-call | tf_op jit(solution)/shard_map/triangular_solve/custom-call.0 | solution.py:17
  (63 shorter events, 40.4 us)
Async XLA Ops:
  1.6 1.4 collective-permute-start
  3.1 8.4 %collective-permute-start.1 = (bf16[1024,128]{0,1:T(8,128)(2,1)S(1)}, bf16[1024,128]{0,1:T(8,128)(2,1)S(1)}, u32[]{:S(2)}, u32[]{:S(2)}) collective-permute-start(bf16[1024,128]{0,1:T(8,128)(2,1)S(1)} %maximum_select_fusion.4), channel_id=1, source_target_pairs={{0,2},{1,3},{2,0},{3,1},{4,6},{5,7},{6,4},{7,5},{8,10},{9,11},{10,... | collective-permute-start | bytes 786440 | tf_op jit(solution)/shard_map/ppermute | solution.py:12
  40.1 92.0 %collective-permute-start.2 = (bf16[16384,128]{0,1:T(8,128)(2,1)}, bf16[16384,128]{0,1:T(8,128)(2,1)S(1)}, u32[]{:S(2)}, u32[]{:S(2)}) collective-permute-start(bf16[16384,128]{0,1:T(8,128)(2,1)} %get-tuple-element.8), channel_id=1, source_target_pairs={{0,4},{1,5},{2,6},{3,7},{4,0},{5,1},{6,2},{7,3},{8,12},{9,13},{10,... | collective-permute-start | bytes 12582920 | tf_op jit(solution)/shard_map/ppermute | solution.py:12
  132.1 5.7 copy-start
  137.9 180.8 %collective-permute-start.3 = (bf16[16384,128]{0,1:T(8,128)(2,1)S(1)}, bf16[16384,128]{0,1:T(8,128)(2,1)}, u32[]{:S(2)}, u32[]{:S(2)}) collective-permute-start(bf16[16384,128]{0,1:T(8,128)(2,1)S(1)} %fusion.14), channel_id=1, source_target_pairs={{0,8},{1,9},{2,10},{3,11},{4,12},{5,13},{6,14},{7,15},{8,0},{9,1},... | collective-permute-start | bytes 12582920 | tf_op jit(solution)/shard_map/ppermute | solution.py:12
  352.7 8.3 %collective-permute-start.4 = (bf16[1024,128]{0,1:T(8,128)(2,1)S(1)}, bf16[1024,128]{0,1:T(8,128)(2,1)S(1)}, u32[]{:S(2)}, u32[]{:S(2)}) collective-permute-start(bf16[1024,128]{0,1:T(8,128)(2,1)S(1)} %select_convert_fusion.1), channel_id=1, source_target_pairs={{0,2},{1,3},{2,0},{3,1},{4,6},{5,7},{6,4},{7,5},{8,10},{9,11},{10,... | collective-permute-start | bytes 786440 | tf_op jit(solution)/shard_map/ppermute | solution.py:12
  361.2 1.4 collective-permute-start.5
  363.0 1.3 collective-permute-start.6
  364.3 4.3 collective-permute-start.7
  368.7 4.3 collective-permute-start.8
  373.0 5.8 collective-permute-start.9
  402.2 1.4 collective-permute-start.10
  403.7 8.4 %collective-permute-start.11 = (bf16[1024,128]{0,1:T(8,128)(2,1)S(1)}, bf16[1024,128]{0,1:T(8,128)(2,1)S(1)}, u32[]{:S(2)}, u32[]{:S(2)}) collective-permute-start(bf16[1024,128]{0,1:T(8,128)(2,1)S(1)} %maximum_select_fusion.5), channel_id=1, source_target_pairs={{0,2},{1,3},{2,0},{3,1},{4,6},{5,7},{6,4},{7,5},{8,10},{9,11},{10,... | collective-permute-start | bytes 786440 | tf_op jit(solution)/shard_map/ppermute | solution.py:12
  440.7 92.0 %collective-permute-start.12 = (bf16[16384,128]{0,1:T(8,128)(2,1)}, bf16[16384,128]{0,1:T(8,128)(2,1)S(1)}, u32[]{:S(2)}, u32[]{:S(2)}) collective-permute-start(bf16[16384,128]{0,1:T(8,128)(2,1)} %get-tuple-element.10), channel_id=1, source_target_pairs={{0,4},{1,5},{2,6},{3,7},{4,0},{5,1},{6,2},{7,3},{8,12},{9,13},{10,... | collective-permute-start | bytes 12582920 | tf_op jit(solution)/shard_map/ppermute | solution.py:12
  537.1 181.4 %collective-permute-start.13 = (bf16[16384,128]{0,1:T(8,128)(2,1)S(1)}, bf16[16384,128]{0,1:T(8,128)(2,1)}, u32[]{:S(2)}, u32[]{:S(2)}) collective-permute-start(bf16[16384,128]{0,1:T(8,128)(2,1)S(1)} %fusion.15), channel_id=1, source_target_pairs={{0,8},{1,9},{2,10},{3,11},{4,12},{5,13},{6,14},{7,15},{8,0},{9,1},... | collective-permute-start | bytes 12582920 | tf_op jit(solution)/shard_map/ppermute | solution.py:12
  756.5 8.3 %collective-permute-start.14 = (bf16[1024,128]{0,1:T(8,128)(2,1)S(1)}, bf16[1024,128]{0,1:T(8,128)(2,1)S(1)}, u32[]{:S(2)}, u32[]{:S(2)}) collective-permute-start(bf16[1024,128]{0,1:T(8,128)(2,1)S(1)} %select_convert_fusion), channel_id=1, source_target_pairs={{0,2},{1,3},{2,0},{3,1},{4,6},{5,7},{6,4},{7,5},{8,10},{9,11},{10,... | collective-permute-start | bytes 786440 | tf_op jit(solution)/shard_map/ppermute | solution.py:12
  764.9 1.4 collective-permute-start.15
  766.7 1.3 collective-permute-start.16
  768.0 4.3 collective-permute-start.17
  772.4 4.3 collective-permute-start.18
  776.7 6.2 collective-permute-start.19
